TPU v7x, 32 devices: a whole 2x2x4 slice. The times are simulated.
32 devices in a mesh: tm: 8 (over y, x, core), row: 4 (over z).
Axes of the slice: x: 2, y: 2, z: 4, core: 2. Of those that a mesh axis runs over, the one named last changes fastest.
Arguments:
- feature: bfloat16 [32, 16, 128, 384], P('tm', 'row'), may hold values from -6 to 6
- conv_weight: bfloat16 [3, 3, 3, 384, 384], replicated, may hold values from -0.0625 to 0.0625
- conv_bias: float32 [384], replicated, may hold values from -3 to 3
- down_weight: bfloat16 [3, 2, 2, 384, 16], replicated, may hold values from -0.09375 to 0.09375
- down_bias: float32 [16], replicated, may hold values from -3 to 3
Outputs:
- tokens: float32 [2048, 64], P(('tm', 'row'))
All inputs are finite; a program needn't handle non-finite values.
Results may differ from a plain program's by a relative error of at most 0.0022.
Values may be sent and summed in bfloat16 or wider, within the bound.
A program may use at most 128 MiB of HBM per device.

v0:
```python
import jax
import jax.numpy as jnp
from jax import lax
from jax.sharding import PartitionSpec as P

Z = 16


def with_halo(block, sides, width):
    for axis, dim in sides:
        count = lax.axis_size(axis)
        forward = [(i, i + 1) for i in range(count - 1)]
        backward = [(target, source) for source, target in forward]
        low = lax.ppermute(
            lax.slice_in_dim(block, block.shape[dim] - width, None, axis=dim), axis, forward
        )
        high = lax.ppermute(lax.slice_in_dim(block, 0, width, axis=dim), axis, backward)
        block = jnp.concatenate([low, block, high], axis=dim)
    return block


def passed_along(shard, axis, by):
    length = lax.axis_size(axis)
    pairs = [(i, i + by) for i in range(length) if 0 <= i + by < length]
    return lax.ppermute(shard, axis, pairs)


def convolve(extended, conv_weight, conv_bias, frames):
    channels = extended.shape[-1]
    height = extended.shape[1] - 2
    width = extended.shape[2]
    total = jnp.zeros((frames * height * width, 3 * channels), jnp.float32)
    for tap_time in range(3):
        for tap_row in range(3):
            slab = extended[tap_time : tap_time + frames, tap_row : tap_row + height].reshape(
                frames * height * width, channels
            )
            mixed = (
                conv_weight[tap_time, tap_row].transpose(1, 0, 2).reshape(channels, 3 * channels)
            )
            total = total + jnp.dot(slab, mixed, preferred_element_type=jnp.float32)
    total = total.reshape(frames * height, width, 3 * channels)
    left_part = total[:, : width - 1, :channels]
    centre = total[:, :, channels : 2 * channels]
    right_part = total[:, 1:, 2 * channels :]
    pre = (
        centre
        + jnp.pad(left_part, ((0, 0), (1, 0), (0, 0)))
        + jnp.pad(right_part, ((0, 0), (0, 1), (0, 0)))
    )
    return (
        jax.nn.silu(pre + conv_bias).astype(jnp.bfloat16).reshape(frames, height, width, channels)
    )


def on_device(feature, conv_weight, conv_bias, down_weight, down_bias):
    channels = feature.shape[-1]
    own_frames = feature.shape[0]
    own_rows = feature.shape[1]
    depth = 2
    banded = with_halo(feature, (("row", 1),), 1)
    earlier = passed_along(banded[own_frames - depth :], "tm", 1)
    extended = jnp.concatenate([earlier, banded], axis=0)
    activated = convolve(extended, conv_weight, conv_bias, own_frames)
    previous = passed_along(activated[own_frames - 1 :], "tm", 1)
    shifted = jnp.concatenate([previous, activated], axis=0)
    lat_frames = own_frames // 2
    lat_rows = own_rows // 2
    lat_cols = feature.shape[2] // 2
    latent = jnp.zeros((lat_frames, lat_rows, lat_cols, Z), jnp.float32)
    for tap_time in range(3):
        part = shifted[tap_time : tap_time + own_frames : 2].reshape(
            lat_frames, lat_rows, 2, lat_cols, 2, channels
        )
        latent = latent + jnp.einsum(
            "fidjek,dekz->fijz", part, down_weight[tap_time], preferred_element_type=jnp.float32
        )
    latent = latent + down_bias
    patch_cols = lat_cols // 2
    mine = (
        latent.reshape(lat_frames, 2, patch_cols, 2, Z)
        .transpose(0, 2, 1, 3, 4)
        .reshape(lat_frames, patch_cols, 4 * Z)
    )
    band = lax.axis_index("row")
    n_bands = lax.axis_size("row")
    frame_range = jnp.arange(lat_frames, dtype=jnp.int32)
    slot_ids = jnp.arange(n_bands * lat_frames, dtype=jnp.int32)
    select = (slot_ids % n_bands == band)[:, None] & (
        (slot_ids // n_bands)[:, None] == frame_range[None, :]
    )
    outgoing = jnp.sum(jnp.where(select[:, :, None, None], mine[None], 0.0), axis=1)
    outgoing = outgoing.reshape(n_bands, lat_frames, patch_cols, 4 * Z)
    incoming = lax.all_to_all(outgoing, "row", split_axis=0, concat_axis=0, tiled=True)
    result = jnp.sum(incoming, axis=0)
    return result.reshape(lat_frames * patch_cols, 4 * Z)


def solution(mesh):
    return jax.shard_map(
        on_device,
        mesh=mesh,
        in_specs=(P("tm", "row", None, None), P(), P(), P(), P()),
        out_specs=P(("tm", "row"), None),
        check_vma=False,
    )
```

profile of v0, /device:TPU:4, one launch (start us, length us, event | category | flops | bytes accessed | tf_op | source)
XLA Modules:
  0.0 121.2 jit_solution(5429505141494148308)
XLA Ops:
  2.1 4.2 %collective-permute-start = (bf16[4,1,128,384]{3,2,1,0:T(8,128)(2,1)}, bf16[4,1,128,384]{3,2,1,0:T(8,128)(2,1)}, u32[]{:S(2)}, u32[]{:S(2)}) collective-permute-start(bf16[4,1,128,384]{3,2,1,0:T(8,128)(2,1)} %get-tuple-element.27), channel_id=1, source_target_pairs={{0,1},{1,2},{2,3},{4,5},{5,6},{6,7},{8,9},{9,10},{10,11},{12,13},{... | collective-permute-start | bytes 1179656 | tf_op jit(solution)/shard_map/ppermute | solution.py:14
  7.6 5.3 %fusion.22 = (bf16[1,1,3,384,384]{4,3,2,1,0:T(8,128)(2,1)S(1)}, bf16[1,1,3,384,384]{4,3,2,1,0:T(8,128)(2,1)}, bf16[1,1,3,384,384]{4,3,2,1,0:T(8,128)(2,1)S(1)}, ...) fusion(bf16[3,3,3,384,384]{4,3,2,1,0:T(8,128)(2,1)} %param.6), kind=kLoop, calls=%fused_computation.58 | loop fusion | bytes 15925248 | tf_op jit(solution)/shard_map/slice | solution.py:39
  12.9 2.3 %copy.64 = bf16[1,1,3,384,384]{3,4,2,1,0:T(8,128)(2,1)} copy(bf16[1,1,3,384,384]{4,3,2,1,0:T(8,128)(2,1)} %get-tuple-element.13) | data formatting | bytes 1769472
  15.2 2.3 %copy.63 = bf16[1,1,3,384,384]{3,4,2,1,0:T(8,128)(2,1)} copy(bf16[1,1,3,384,384]{4,3,2,1,0:T(8,128)(2,1)} %get-tuple-element.14) | data formatting | bytes 1769472
  17.5 2.3 %copy.65 = bf16[1,1,3,384,384]{3,4,2,1,0:T(8,128)(2,1)} copy(bf16[1,1,3,384,384]{4,3,2,1,0:T(8,128)(2,1)} %get-tuple-element.12) | data formatting | bytes 1769472
  21.9 2.2 %copy.67 = bf16[1,1,3,384,384]{3,4,2,1,0:T(8,128)(2,1)} copy(bf16[1,1,3,384,384]{4,3,2,1,0:T(8,128)(2,1)S(1)} %get-tuple-element.10) | data formatting | bytes 1769472
  26.2 2.3 %copy.69 = bf16[1,1,3,384,384]{3,4,2,1,0:T(8,128)(2,1)S(1)} copy(bf16[1,1,3,384,384]{4,3,2,1,0:T(8,128)(2,1)S(1)} %get-tuple-element.7) | data formatting | bytes 1769472
  28.5 2.6 %copy.70 = bf16[1,1,3,384,384]{3,4,2,1,0:T(8,128)(2,1)S(1)} copy(bf16[1,1,3,384,384]{4,3,2,1,0:T(8,128)(2,1)} %get-tuple-element.8) | data formatting | bytes 1769472
  31.1 2.3 %copy.71 = bf16[1,1,3,384,384]{3,4,2,1,0:T(8,128)(2,1)} copy(bf16[1,1,3,384,384]{4,3,2,1,0:T(8,128)(2,1)} %get-tuple-element.15) | data formatting | bytes 1769472
  34.5 2.9 %pad_maximum_fusion.2 = (bf16[4,4,128,384]{3,2,1,0:T(8,128)(2,1)S(1)}, bf16[4,4,128,384]{3,2,1,0:T(8,128)(2,1)}, bf16[4,6,128,384]{3,2,1,0:T(8,128)(2,1)S(1)}) fusion(bf16[4,4,128,384]{3,2,1,0:T(8,128)(2,1)S(1)} %copy-done, bf16[4,1,128,384]{3,2,1,0:T(8,128)(2,1)} %collective-permute-done, bf16[4,1,128,384]{3,2,1,0:T(8,128)(2,1)} %collective-permute-done.1, ...), kind=kLoop, calls=%fused_computation.27 | loop fusion | flops 6291456 | bytes 7077888 | tf_op jit(solution)/shard_map/concatenate | solution.py:18
  40.6 5.1 %fusion.27 = f32[2048,1152]{1,0:T(8,128)} fusion(bf16[2048,384]{1,0:T(8,128)(2,1)S(1)} %bitcast.133, bf16[384,1152]{0,1:T(8,128)(2,1)S(1)} %bitcast.139), kind=kOutput, calls=%fused_computation.63 | convolution fusion | flops 1811939328 | bytes 11894784 | tf_op jit(solution)/shard_map/dot_general | solution.py:41
  45.7 5.1 %fusion.26 = f32[2048,1152]{1,0:T(8,128)} fusion(bf16[2048,384]{1,0:T(8,128)(2,1)S(1)} %bitcast.134, bf16[384,1152]{0,1:T(8,128)(2,1)S(1)} %bitcast.138), kind=kOutput, calls=%fused_computation.62 | convolution fusion | flops 1811939328 | bytes 11894784 | tf_op jit(solution)/shard_map/dot_general | solution.py:41
  50.9 6.2 %collective-permute-done.2 = bf16[2,6,128,384]{3,2,1,0:T(8,128)(2,1)S(1)} collective-permute-done((bf16[2,6,128,384]{3,2,1,0:T(8,128)(2,1)S(1)}, bf16[2,6,128,384]{3,2,1,0:T(8,128)(2,1)S(1)}, u32[]{:S(2)}, u32[]{:S(2)}) %collective-permute-start.2) | collective-permute-done | bytes 1179680 | tf_op jit(solution)/shard_map/ppermute | solution.py:25
  58.4 2.8 %fusion.25 = f32[2048,1152]{1,0:T(8,128)S(1)} fusion(bf16[2048,384]{1,0:T(8,128)(2,1)S(1)} %bitcast.135, bf16[384,1152]{0,1:T(8,128)(2,1)S(1)} %bitcast.137), kind=kOutput, calls=%fused_computation.61 | convolution fusion | flops 1811939328 | bytes 11894784 | tf_op jit(solution)/shard_map/dot_general | solution.py:41
  61.2 2.8 %convolution_add_fusion.5 = f32[2048,1152]{1,0:T(8,128)S(1)} fusion(f32[2048,1152]{1,0:T(8,128)S(1)} %fusion.25, bf16[2048,384]{1,0:T(8,128)(2,1)S(1)} %bitcast.132, bf16[384,1152]{0,1:T(8,128)(2,1)S(1)} %bitcast.145), kind=kOutput, calls=%fused_computation.5 | convolution fusion | flops 1814298624 | bytes 21331968 | tf_op jit(solution)/shard_map/dot_general | solution.py:41
  64.0 2.8 %convolution_add_fusion.4 = f32[2048,1152]{1,0:T(8,128)S(1)} fusion(f32[2048,1152]{1,0:T(8,128)S(1)} %convolution_add_fusion.5, bf16[2048,384]{1,0:T(8,128)(2,1)S(1)} %bitcast.131, bf16[384,1152]{0,1:T(8,128)(2,1)S(1)} %bitcast.144), kind=kOutput, calls=%fused_computation.4 | convolution fusion | flops 1814298624 | bytes 21331968 | tf_op jit(solution)/shard_map/dot_general | solution.py:41
  66.8 4.1 %convolution_add_fusion.3 = f32[2048,1152]{1,0:T(8,128)S(1)} fusion(f32[2048,1152]{1,0:T(8,128)S(1)} %convolution_add_fusion.4, bf16[2048,384]{1,0:T(8,128)(2,1)S(1)} %bitcast.130, bf16[384,1152]{0,1:T(8,128)(2,1)} %bitcast.143), kind=kOutput, calls=%fused_computation.3 | convolution fusion | flops 1814298624 | bytes 21331968 | tf_op jit(solution)/shard_map/dot_general | solution.py:41
  70.9 4.4 %convolution_add_fusion.2 = f32[2048,1152]{1,0:T(8,128)S(1)} fusion(f32[2048,1152]{1,0:T(8,128)S(1)} %convolution_add_fusion.3, bf16[2048,384]{1,0:T(8,128)(2,1)S(1)} %bitcast.129, bf16[384,1152]{0,1:T(8,128)(2,1)} %bitcast.142), kind=kOutput, calls=%fused_computation.2 | convolution fusion | flops 1814298624 | bytes 21331968 | tf_op jit(solution)/shard_map/dot_general | solution.py:41
  75.4 3.0 %convolution_add_fusion.1 = f32[2048,1152]{1,0:T(8,128)S(1)} fusion(f32[2048,1152]{1,0:T(8,128)S(1)} %convolution_add_fusion.2, bf16[2048,384]{1,0:T(8,128)(2,1)S(1)} %bitcast.128, bf16[384,1152]{0,1:T(8,128)(2,1)S(1)} %bitcast.140), kind=kOutput, calls=%fused_computation.1 | convolution fusion | flops 1814298624 | bytes 21331968 | tf_op jit(solution)/shard_map/dot_general | solution.py:41
  78.4 10.5 %convolution_add_fusion = f32[2048,1152]{1,0:T(8,128)} fusion(bf16[2048,384]{1,0:T(8,128)(2,1)S(1)} %bitcast.136, bf16[384,1152]{0,1:T(8,128)(2,1)S(1)} %bitcast.141, f32[2048,1152]{1,0:T(8,128)} %fusion.27, f32[2048,1152]{1,0:T(8,128)S(1)} %convolution_add_fusion.1, f32[2048,1152]{1,0:T(8,128)} %fusion.26), kind=kOutput, calls=%fused_computation | convolution fusion | flops 1819017216 | bytes 40206336 | tf_op jit(solution)/shard_map/dot_general | solution.py:41
  88.9 3.5 %fusion.21 = (f32[16,127,384]{2,1,0:T(8,128)S(1)}, f32[16,127,384]{2,1,0:T(8,128)S(1)}) fusion(f32[16,128,1152]{2,1,0:T(8,128)} %bitcast.124), kind=kLoop, calls=%fused_computation.57 | loop fusion | bytes 12484608 | tf_op jit(solution)/shard_map/slice | solution.py:43
  92.4 3.1 %multiply_convert_fusion = bf16[16,128,384]{2,1,0:T(8,128)(2,1)S(1)} fusion(f32[16,128,1152]{2,1,0:T(8,128)} %bitcast.125, f32[16,127,384]{2,1,0:T(8,128)S(1)} %get-tuple-element.6, f32[16,127,384]{2,1,0:T(8,128)S(1)} %get-tuple-element.5, f32[384]{0:T(512)S(1)} %copy-done.7), kind=kLoop, calls=%fused_computation.19 | loop fusion | flops 6291456 | bytes 10962432 | tf_op jit(solution)/shard_map/convert_element_type | solution.py:52
  100.2 5.4 %collective-permute-done.3 = bf16[1,4,128,384]{3,2,1,0:T(8,128)(2,1)S(1)} collective-permute-done((bf16[1,4,128,384]{3,2,1,0:T(8,128)(2,1)S(1)}, bf16[1,4,128,384]{3,2,1,0:T(8,128)(2,1)S(1)}, u32[]{:S(2)}, u32[]{:S(2)}) %collective-permute-start.3) | collective-permute-done | bytes 393248 | tf_op jit(solution)/shard_map/ppermute | solution.py:25
  107.7 11.5 %all_to_all.5 = f32[4,1,4096]{2,1,0:T(1,128)S(1)} all-to-all(f32[4,1,4096]{2,1,0:T(1,128)S(1)} %reshape.172), channel_id=1, replica_groups=mesh['tm'=8,'row'=4] {'row'}, dimensions={0} | all-to-all | bytes 131072 | tf_op jit(solution)/shard_map/all_to_all | solution.py:94
  (54 shorter events, 22.0 us)
Async XLA Ops:
  2.1 31.4 %collective-permute-start = (bf16[4,1,128,384]{3,2,1,0:T(8,128)(2,1)}, bf16[4,1,128,384]{3,2,1,0:T(8,128)(2,1)}, u32[]{:S(2)}, u32[]{:S(2)}) collective-permute-start(bf16[4,1,128,384]{3,2,1,0:T(8,128)(2,1)} %get-tuple-element.27), channel_id=1, source_target_pairs={{0,1},{1,2},{2,3},{4,5},{5,6},{6,7},{8,9},{9,10},{10,11},{12,13},{... | collective-permute-start | bytes 1179656 | tf_op jit(solution)/shard_map/ppermute | solution.py:14
  6.3 28.2 %collective-permute-start.1 = (bf16[4,1,128,384]{3,2,1,0:T(8,128)(2,1)}, bf16[4,1,128,384]{3,2,1,0:T(8,128)(2,1)}, u32[]{:S(2)}, u32[]{:S(2)}) collective-permute-start(bf16[4,1,128,384]{3,2,1,0:T(8,128)(2,1)} %get-tuple-element.28), channel_id=1, source_target_pairs={{1,0},{2,1},{3,2},{5,4},{6,5},{7,6},{9,8},{10,9},{11,10},{13,12},{... | collective-permute-start | bytes 1179656 | tf_op jit(solution)/shard_map/ppermute | solution.py:17
  28.5 6.0 %copy-start = (bf16[4,4,128,384]{3,2,1,0:T(8,128)(2,1)S(1)}, bf16[4,4,128,384]{3,2,1,0:T(8,128)(2,1)}, u32[]{:S(2)}) copy-start(bf16[4,4,128,384]{3,2,1,0:T(8,128)(2,1)} %param.5) | copy-start | bytes 4718596
  38.6 18.4 %collective-permute-start.2 = (bf16[2,6,128,384]{3,2,1,0:T(8,128)(2,1)S(1)}, bf16[2,6,128,384]{3,2,1,0:T(8,128)(2,1)S(1)}, u32[]{:S(2)}, u32[]{:S(2)}) collective-permute-start(bf16[2,6,128,384]{3,2,1,0:T(8,128)(2,1)S(1)} %slice.126), channel_id=1, source_target_pairs={{0,4},{4,8},{8,12},{12,16},{16,20},{20,24},{24,28},{1,5},{5,9},{9,... | collective-permute-start | bytes 3538952 | tf_op jit(solution)/shard_map/ppermute | solution.py:25
  50.9 7.6 %copy-start.2 = (bf16[1,1,3,384,384]{3,4,2,1,0:T(8,128)(2,1)S(1)}, bf16[1,1,3,384,384]{3,4,2,1,0:T(8,128)(2,1)}, u32[]{:S(2)}) copy-start(bf16[1,1,3,384,384]{3,4,2,1,0:T(8,128)(2,1)} %copy.64) | copy-start | bytes 2654212
  58.4 2.8 %copy-start.6 = (bf16[1,1,3,384,384]{3,4,2,1,0:T(8,128)(2,1)S(1)}, bf16[1,1,3,384,384]{3,4,2,1,0:T(8,128)(2,1)}, u32[]{:S(2)}) copy-start(bf16[1,1,3,384,384]{3,4,2,1,0:T(8,128)(2,1)} %copy.63) | copy-start | bytes 2654212
  61.2 2.8 %copy-start.5 = (bf16[1,1,3,384,384]{3,4,2,1,0:T(8,128)(2,1)S(1)}, bf16[1,1,3,384,384]{3,4,2,1,0:T(8,128)(2,1)}, u32[]{:S(2)}) copy-start(bf16[1,1,3,384,384]{3,4,2,1,0:T(8,128)(2,1)} %copy.65) | copy-start | bytes 2654212
  70.9 4.4 %copy-start.3 = (bf16[1,1,3,384,384]{3,4,2,1,0:T(8,128)(2,1)S(1)}, bf16[1,1,3,384,384]{3,4,2,1,0:T(8,128)(2,1)}, u32[]{:S(2)}) copy-start(bf16[1,1,3,384,384]{3,4,2,1,0:T(8,128)(2,1)} %copy.68) | copy-start | bytes 2654212
  75.4 3.0 %copy-start.1 = (bf16[4,4,128,384]{3,2,1,0:T(8,128)(2,1)S(1)}, bf16[4,4,128,384]{3,2,1,0:T(8,128)(2,1)}, u32[]{:S(2)}) copy-start(bf16[4,4,128,384]{3,2,1,0:T(8,128)(2,1)} %get-tuple-element.25) | copy-start | bytes 4718596
  75.4 3.0 %copy-start.4 = (bf16[1,1,3,384,384]{3,4,2,1,0:T(8,128)(2,1)S(1)}, bf16[1,1,3,384,384]{3,4,2,1,0:T(8,128)(2,1)}, u32[]{:S(2)}) copy-start(bf16[1,1,3,384,384]{3,4,2,1,0:T(8,128)(2,1)} %copy.71) | copy-start | bytes 2654212
  88.9 3.6 %copy-start.7 = (f32[384]{0:T(512)S(1)}, f32[384]{0:T(512)}, u32[]{:S(2)}) copy-start(f32[384]{0:T(512)} %param.7) | copy-start | bytes 4612
  95.6 10.0 %collective-permute-start.3 = (bf16[1,4,128,384]{3,2,1,0:T(8,128)(2,1)S(1)}, bf16[1,4,128,384]{3,2,1,0:T(8,128)(2,1)S(1)}, u32[]{:S(2)}, u32[]{:S(2)}) collective-permute-start(bf16[1,4,128,384]{3,2,1,0:T(8,128)(2,1)S(1)} %slice_bitcast_fusion), channel_id=1, source_target_pairs={{0,4},{4,8},{8,12},{12,16},{16,20},{20,24},{24,28},{1,5},{5,9},{9,... | collective-permute-start | bytes 1179656 | tf_op jit(solution)/shard_map/ppermute | solution.py:25
  97.7 1.7 %copy-start.8 = (bf16[3,2,2,384,16]{3,4,2,1,0:T(8,128)(2,1)S(1)}, bf16[3,2,2,384,16]{3,4,2,1,0:T(8,128)(2,1)}, u32[]{:S(2)}) copy-start(bf16[3,2,2,384,16]{3,4,2,1,0:T(8,128)(2,1)} %param.8) | copy-start | bytes 442372
  105.8 0.9 copy-start.9
where the time goes:
time: 122 us; the launch traced here: 121 us
  matrix products  41.8 us (34%)
  local copies, waits for them, and re-layouts  37.5 us (31%)
  waiting for transfers between devices  11.6 us (10%)
  blocking collectives  11.5 us (9%)
  starting transfers between devices  9.37 us (8%)
  other arithmetic  9.23 us (8%)
    dot_general x9, matrix products, convolve(): total = total + jnp.dot(slab, mixed, preferred_element_type=jnp.float32)  40.5 us
    unnamed x32, local copies, waits for them, and re-layouts  21.8 us
    ppermute x2, waiting for transfers between devices, passed_along(): return lax.ppermute(shard, axis, pairs)  11.6 us
    all_to_all x1, blocking collectives, on_device(): lax.all_to_all(outgoing, 'row', split_axis=0, concat_axis=0, tiled=True)  11.5 us
    slice x1, local copies, waits for them, and re-layouts, convolve(): conv_weight[tap_time, tap_row].transpose(1, 0, 2)  5.3 us
    ppermute x1, starting transfers between devices, with_halo(): lax.ppermute(lax.slice_in_dim(block, block.shape[dim] - width, None, axis...  4.25 us
    ppermute x2, starting transfers between devices, passed_along(): return lax.ppermute(shard, axis, pairs)  3.84 us
    slice x1, local copies, waits for them, and re-layouts, convolve(): left_part = total[:, :width - 1, :channels]  3.54 us
  transfers between devices with their start and end apart: 4, of which 2 were waited for; matrix products, arithmetic and copies ran while one was open for 33% of the time, Pallas kernels for 0%

commit v1 on v0

v1 whole, which is shorter than its diff:
```python
import functools

import jax
import jax.numpy as jnp
from jax import lax
from jax.experimental import pallas as pl
from jax.experimental.pallas import tpu as pltpu
from jax.sharding import PartitionSpec as P

MESH = pl.DeviceIdType.MESH
F32 = jnp.float32
BF16 = jnp.bfloat16


def kernel(
    n_tm, n_row,
    x_ref, cw_ref, cb_ref, dw_ref, db_ref,
    out_ref,
    xs, w, acc, act, wd, s_ref, tx, rx, cx,
    w_sem, x_sem, send_sem, recv_sem, tx_sem, rx_sem, cx_sem,
):
    frames, rows, cols, chans = x_ref.shape
    lat = frames // 2
    tm = lax.axis_index("tm")
    row = lax.axis_index("row")
    up_ok, down_ok = row > 0, row < n_row - 1
    next_ok, prev_ok = tm < n_tm - 1, tm > 0

    last = pl.ds(frames - 2, 2)
    halos = [
        (x_ref.at[:, 0], xs.at[pl.ds(2, frames), rows + 1], 0, -1, up_ok, down_ok),
        (x_ref.at[:, rows - 1], xs.at[pl.ds(2, frames), 0], 0, 1, down_ok, up_ok),
        (x_ref.at[last], xs.at[pl.ds(0, 2), pl.ds(1, rows)], 1, 0, next_ok, prev_ok),
        (x_ref.at[last, 0], xs.at[pl.ds(0, 2), rows + 1], 1, -1, next_ok & up_ok, prev_ok & down_ok),
        (x_ref.at[last, rows - 1], xs.at[pl.ds(0, 2), 0], 1, 1, next_ok & down_ok, prev_ok & up_ok),
    ]

    def halo_copy(k):
        src, dst, dt, dr, _, _ = halos[k]
        return pltpu.make_async_remote_copy(
            src_ref=src, dst_ref=dst, send_sem=send_sem.at[k], recv_sem=recv_sem.at[k],
            device_id={"tm": tm + dt, "row": row + dr}, device_id_type=MESH,
        )

    def owner_of(f):
        unit = f * n_row + row
        return unit // lat, unit % lat

    barrier = pltpu.get_barrier_semaphore()

    def greet(dt, dr, when):
        @pl.when(when)
        def _():
            pl.semaphore_signal(
                barrier, inc=1, device_id={"tm": tm + dt, "row": row + dr}, device_id_type=MESH
            )

    for _, _, dt, dr, _, comes in halos:
        greet(-dt, -dr, comes)
    for slot in range(lat):
        unit = row * lat + slot
        source = unit % n_row
        greet(0, source - row, source != row)
        greet(-1, source - row, prev_ok & (unit < n_row))

    x_copy = pltpu.make_async_copy(x_ref, xs.at[pl.ds(2, frames), pl.ds(1, rows)], x_sem)
    x_copy.start()
    w_copies = []
    for a in range(3):
        for b in range(3):
            for c in range(3):
                w_copies.append(
                    pltpu.make_async_copy(
                        cw_ref.at[a, b, c],
                        w.at[pl.ds((3 * a + b) * chans, chans), pl.ds(c * chans, chans)],
                        w_sem.at[9 * a + 3 * b + c],
                    )
                )
                w_copies[-1].start()

    targets = [goes for _, _, _, _, goes, _ in halos] + [next_ok]
    targets += [owner_of(f)[0] != row for f in range(lat)]
    pl.semaphore_wait(barrier, sum(jnp.where(goes, 1, 0) for goes in targets))

    for k in range(5):
        @pl.when(halos[k][4])
        def _(k=k):
            halo_copy(k).start()

    @pl.when(row == 0)
    def _():
        xs[:, 0] = jnp.zeros((frames + 2, cols, chans), BF16)

    @pl.when(row == n_row - 1)
    def _():
        xs[:, rows + 1] = jnp.zeros((frames + 2, cols, chans), BF16)

    @pl.when(tm == 0)
    def _():
        xs[0:2] = jnp.zeros((2, rows + 2, cols, chans), BF16)

    zi = lax.broadcasted_iota(jnp.int32, (16, 128), 0)
    li = lax.broadcasted_iota(jnp.int32, (16, 128), 1)
    spread = [((li % 16 == zi) & (li // 64 == dx)).astype(F32).astype(BF16) for dx in range(2)]
    for a in range(3):
        for dy in range(2):
            part = sum(
                lax.dot_general(
                    dw_ref[a, dy, dx], spread[dx], (((0,), (0,)), ((), ())),
                    preferred_element_type=F32,
                )
                for dx in range(2)
            )
            wd[a * chans : (a + 1) * chans, dy * 128 : (dy + 1) * 128] = part.astype(BF16)

    x_copy.wait()
    for copy in w_copies:
        copy.wait()

    pairs = frames // 2
    early = pairs - 1
    row_id = lax.broadcasted_iota(jnp.int32, (cols, chans), 0)

    def await_halo(k, when):
        @pl.when(when & halos[k][5])
        def _():
            halo_copy(k).wait_recv()

    def conv_step(step, _):
        await_halo(0, step == early)
        await_halo(1, step == early)
        await_halo(2, step == 2 * early)
        await_halo(3, step == 2 * early + 1)
        await_halo(4, step == 2 * early + 1)
        is_late = step >= 2 * early
        outer = jnp.where(is_late, step - 2 * early, (step >= early).astype(jnp.int32))
        pair = jnp.where(is_late, 0, step - outer * early + 1)
        first = 2 * pair
        places = [(df, i) for df in range(2) for i in range(2)]
        spots = [(first + df, 1 - outer if i == 0 else 2 + outer) for df, i in places]
        pieces = []
        for a in range(3):
            for b in range(3):
                pieces.append(jnp.concatenate([xs[f + a, i + b] for f, i in spots], axis=0))
        lhs = jnp.concatenate(pieces, axis=1)
        acc[:, : 2 * chans] = jnp.dot(lhs, w[:, : 2 * chans], preferred_element_type=F32)
        acc[:, 2 * chans :] = jnp.dot(lhs, w[:, 2 * chans :], preferred_element_type=F32)
        for n, (f, i) in enumerate(spots):
            span = slice(n * cols, (n + 1) * cols)
            left = pltpu.roll(acc[span, :chans], 1, 0)
            right = pltpu.roll(acc[span, 2 * chans :], cols - 1, 0)
            pre = acc[span, chans : 2 * chans] + cb_ref[...]
            pre += jnp.where(row_id == 0, 0.0, left)
            pre += jnp.where(row_id == cols - 1, 0.0, right)
            act[f, i] = (pre / (1.0 + jnp.exp(-pre))).astype(BF16)
        return 0

    lax.fori_loop(0, 2 * pairs, conv_step, 0)

    lane = lax.broadcasted_iota(jnp.int32, (cols // 4, 128), 1)

    def project(parts):
        lhs = jnp.concatenate([act[f].reshape(rows * cols, chans) for f, _ in parts], axis=1)
        low = parts[0][1] * chans
        weights = wd[low : low + len(parts) * chans]
        both = jnp.dot(lhs, weights, preferred_element_type=F32)
        s_ref[0] = both[:, :128]
        s_ref[1] = both[:, 128:]
        even = jnp.zeros((cols // 4, 128), F32)
        odd = jnp.zeros((cols // 4, 128), F32)
        for block in range(4):
            dyo, dxo = block // 2, block % 2
            sums = []
            for dx in range(2):
                sums.append(sum(
                    s_ref[dy, pl.ds((2 * dyo + dy) * cols + 2 * dxo + dx, cols // 4, stride=4), :]
                    for dy in range(2)
                ))
            even = jnp.where(lane // 16 == block, sums[0], even)
            odd = jnp.where(lane // 16 == block + 4, sums[1], odd)
        return even + pltpu.roll(odd, 64, 1)

    def unit_copy(f):
        owner, slot = owner_of(f)
        return pltpu.make_async_remote_copy(
            src_ref=tx.at[f], dst_ref=rx.at[slot], send_sem=tx_sem.at[f], recv_sem=rx_sem.at[slot],
            device_id={"tm": tm, "row": owner}, device_id_type=MESH,
        )

    def tail_copy():
        owner, slot = owner_of(0)
        return pltpu.make_async_remote_copy(
            src_ref=tx.at[lat], dst_ref=cx.at[slot], send_sem=tx_sem.at[lat],
            recv_sem=cx_sem.at[slot],
            device_id={"tm": tm + 1, "row": owner}, device_id_type=MESH,
        )

    tx[lat] = project([(frames - 1, 0)])

    @pl.when(next_ok)
    def _():
        tail_copy().start()

    for f in range(lat):
        if f == 0:
            tokens = project([(0, 1), (1, 2)])
        else:
            tokens = project([(2 * f - 1, 0), (2 * f, 1), (2 * f + 1, 2)])
        owner, slot = owner_of(f)
        tx[f] = tokens

        @pl.when(owner == row)
        def _():
            rx[slot] = tokens

        @pl.when(owner != row)
        def _():
            unit_copy(f).start()

    bias = jnp.concatenate([db_ref[...]] * 4, axis=1)
    quarter = cols // 4
    for slot in range(lat):
        unit = row * lat + slot

        @pl.when(unit % n_row != row)
        def _():
            pltpu.make_async_remote_copy(
                src_ref=tx.at[0], dst_ref=rx.at[slot], send_sem=tx_sem.at[0],
                recv_sem=rx_sem.at[slot],
                device_id={"tm": tm, "row": unit % n_row}, device_id_type=MESH,
            ).wait_recv()

        out_ref[slot * quarter : (slot + 1) * quarter, :] = rx[slot][:, :64] + bias

        @pl.when(prev_ok & (unit < n_row))
        def _():
            pltpu.make_async_remote_copy(
                src_ref=tx.at[lat], dst_ref=cx.at[slot], send_sem=tx_sem.at[lat],
                recv_sem=cx_sem.at[slot],
                device_id={"tm": tm - 1, "row": unit % n_row}, device_id_type=MESH,
            ).wait_recv()
            out_ref[slot * quarter : (slot + 1) * quarter, :] += cx[slot][:, :64]

    for k in range(5):
        @pl.when(halos[k][4])
        def _(k=k):
            halo_copy(k).wait_send()

    @pl.when(next_ok)
    def _():
        tail_copy().wait_send()

    for f in range(lat):
        @pl.when(owner_of(f)[0] != row)
        def _(f=f):
            unit_copy(f).wait_send()


def on_device(n_tm, n_row, feature, conv_weight, conv_bias, down_weight, down_bias):
    frames, rows, cols, chans = feature.shape
    lat = frames // 2
    vmem = pl.BlockSpec(memory_space=pltpu.VMEM)
    anywhere = pl.BlockSpec(memory_space=pl.ANY)
    flops = 2 * frames * rows * cols * 27 * chans * chans
    return pl.pallas_call(
        functools.partial(kernel, n_tm, n_row),
        out_shape=jax.ShapeDtypeStruct((lat * cols // 4, 64), F32),
        in_specs=[anywhere, anywhere, vmem, vmem, vmem],
        out_specs=vmem,
        scratch_shapes=[
            pltpu.VMEM((frames + 2, rows + 2, cols, chans), BF16),
            pltpu.VMEM((9 * chans, 3 * chans), BF16),
            pltpu.VMEM((4 * cols, 3 * chans), F32),
            pltpu.VMEM((frames, rows, cols, chans), BF16),
            pltpu.VMEM((3 * chans, 256), BF16),
            pltpu.VMEM((2, rows * cols, 128), F32),
            pltpu.VMEM((lat + 1, cols // 4, 128), F32),
            pltpu.VMEM((lat, cols // 4, 128), F32),
            pltpu.VMEM((lat, cols // 4, 128), F32),
            pltpu.SemaphoreType.DMA((27,)),
            pltpu.SemaphoreType.DMA,
            pltpu.SemaphoreType.DMA((5,)),
            pltpu.SemaphoreType.DMA((5,)),
            pltpu.SemaphoreType.DMA((lat + 1,)),
            pltpu.SemaphoreType.DMA((lat,)),
            pltpu.SemaphoreType.DMA((lat,)),
        ],
        compiler_params=pltpu.CompilerParams(
            collective_id=0, has_side_effects=True, vmem_limit_bytes=56 * 1024 * 1024
        ),
        cost_estimate=pl.CostEstimate(flops=flops, bytes_accessed=12 << 20, transcendentals=0),
    )(feature, conv_weight, conv_bias.reshape(1, -1), down_weight.swapaxes(3, 4), down_bias.reshape(1, -1))


def solution(mesh):
    return jax.shard_map(
        functools.partial(on_device, mesh.shape["tm"], mesh.shape["row"]),
        mesh=mesh,
        in_specs=(P("tm", "row", None, None), P(), P(), P(), P()),
        out_specs=P(("tm", "row"), None),
        check_vma=False,
    )
```

time: 122 us -> 38.5 us (0.32)
  the two profiles are of different devices: /device:TPU:4 before, /device:TPU:0 now
where the time goes in v1:
time: 38.5 us; the launch traced here: 38.3 us
  Pallas kernels  35.7 us (93%)
  local copies, waits for them, and re-layouts  2.62 us (7%)
    pallas_call x1, Pallas kernels, on_device(): pl.pallas_call(functools.partial(kernel, n_tm, n_row), out_shape=jax.Shap...  35.7 us
    unnamed x1, local copies, waits for them, and re-layouts  1.38 us
    reshape x1, local copies, waits for them, and re-layouts, on_device(): conv_bias.reshape(1, -1)  1.24 us

profile of v1, /device:TPU:0, one launch (start us, length us, event | category | flops | bytes accessed | tf_op | source)
XLA Modules:
  0.0 38.3 jit_solution(6621380362870963888)
XLA Ops:
  0.0 1.2 %reshape.6.cb_ref = f32[1,384]{1,0:T(1,128)} reshape(f32[384]{0:T(512)} %param.7) | data formatting | bytes 3072 | tf_op jit(solution)/shard_map/reshape | solution.py:292
  1.2 35.7 %shard_map.55 = f32[64,64]{1,0:T(8,128)} custom-call(bf16[4,4,128,384]{3,2,1,0:T(8,128)(2,1)} %x_ref.1, bf16[3,3,3,384,384]{4,3,2,1,0:T(8,128)(2,1)} %cw_ref.1, f32[1,384]{1,0:T(1,128)} %reshape.6.cb_ref, bf16[3,2,2,16,384]{4,3,2,1,0:T(8,128)(2,1)} %bitcast.2, f32[1,16]{1,0:T(1,128)} %bitcast.3), custom_call_target="tpu_custom_call" | custom-call | flops 16307453952 | bytes 12582912 | tf_op jit(solution)/shard_map/pallas_call | solution.py:265
  36.9 1.4 %copy.7 = f32[64,64]{1,0:T(8,128)} copy(f32[64,64]{1,0:T(8,128)} %shard_map.55) | data formatting | bytes 32768

commit v2 on v1

--- a/solution.py
+++ b/solution.py
@@ -16,7 +16,7 @@
     n_tm, n_row,
     x_ref, cw_ref, cb_ref, dw_ref, db_ref,
     out_ref,
-    xs, w, acc, act, wd, s_ref, tx, rx, cx,
+    xs, w, acc_a, acc_b, hold, act, wd, s_ref, tx, rx, cx,
     w_sem, x_sem, send_sem, recv_sem, tx_sem, rx_sem, cx_sem,
 ):
     frames, rows, cols, chans = x_ref.shape
@@ -76,13 +76,15 @@
                         w_sem.at[9 * a + 3 * b + c],
                     )
                 )
-                w_copies[-1].start()
+
+    for copy in w_copies[18:] + w_copies[:18]:
+        copy.start()
 
     targets = [goes for _, _, _, _, goes, _ in halos] + [next_ok]
     targets += [owner_of(f)[0] != row for f in range(lat)]
     pl.semaphore_wait(barrier, sum(jnp.where(goes, 1, 0) for goes in targets))
 
-    for k in range(5):
+    for k in range(3):
         @pl.when(halos[k][4])
         def _(k=k):
             halo_copy(k).start()
@@ -114,48 +116,75 @@
             wd[a * chans : (a + 1) * chans, dy * 128 : (dy + 1) * 128] = part.astype(BF16)
 
     x_copy.wait()
-    for copy in w_copies:
-        copy.wait()
 
     pairs = frames // 2
-    early = pairs - 1
     row_id = lax.broadcasted_iota(jnp.int32, (cols, chans), 0)
-
-    def await_halo(k, when):
-        @pl.when(when & halos[k][5])
+    bias_row = cb_ref[...].reshape(1, chans)
+
+    def await_halo(k):
+        @pl.when(halos[k][5])
         def _():
             halo_copy(k).wait_recv()
 
-    def conv_step(step, _):
-        await_halo(0, step == early)
-        await_halo(1, step == early)
-        await_halo(2, step == 2 * early)
-        await_halo(3, step == 2 * early + 1)
-        await_halo(4, step == 2 * early + 1)
-        is_late = step >= 2 * early
-        outer = jnp.where(is_late, step - 2 * early, (step >= early).astype(jnp.int32))
-        pair = jnp.where(is_late, 0, step - outer * early + 1)
-        first = 2 * pair
-        places = [(df, i) for df in range(2) for i in range(2)]
-        spots = [(first + df, 1 - outer if i == 0 else 2 + outer) for df, i in places]
+    def spots_of(pair, outer):
+        picked = (0, rows - 1) if outer else (1, rows - 2)
+        return [(2 * pair + df, i) for df in range(2) for i in picked]
+
+    def gathered(spots, taps):
         pieces = []
-        for a in range(3):
+        for a in taps:
             for b in range(3):
                 pieces.append(jnp.concatenate([xs[f + a, i + b] for f, i in spots], axis=0))
-        lhs = jnp.concatenate(pieces, axis=1)
-        acc[:, : 2 * chans] = jnp.dot(lhs, w[:, : 2 * chans], preferred_element_type=F32)
-        acc[:, 2 * chans :] = jnp.dot(lhs, w[:, 2 * chans :], preferred_element_type=F32)
+        return jnp.concatenate(pieces, axis=1)
+
+    def multiply(into, spots, taps, plus=None):
+        lhs = gathered(spots, taps)
+        span = slice(taps[0] * 3 * chans, (taps[-1] + 1) * 3 * chans)
+        for lanes in (slice(0, 2 * chans), slice(2 * chans, 3 * chans)):
+            part = jnp.dot(lhs, w[span, lanes], preferred_element_type=F32)
+            into[:, lanes] = part if plus is None else part + plus[:, lanes]
+
+    def activate(source, spots):
         for n, (f, i) in enumerate(spots):
             span = slice(n * cols, (n + 1) * cols)
-            left = pltpu.roll(acc[span, :chans], 1, 0)
-            right = pltpu.roll(acc[span, 2 * chans :], cols - 1, 0)
-            pre = acc[span, chans : 2 * chans] + cb_ref[...]
+            left = pltpu.roll(source[span, :chans], 1, 0)
+            right = pltpu.roll(source[span, 2 * chans :], cols - 1, 0)
+            pre = source[span, chans : 2 * chans] + bias_row
             pre += jnp.where(row_id == 0, 0.0, left)
             pre += jnp.where(row_id == cols - 1, 0.0, right)
-            act[f, i] = (pre / (1.0 + jnp.exp(-pre))).astype(BF16)
-        return 0
-
-    lax.fori_loop(0, 2 * pairs, conv_step, 0)
+            half = 0.5 * pre
+            act[f, i] = (half + half * jnp.tanh(half)).astype(BF16)
+
+    for copy in w_copies[18:]:
+        copy.wait()
+    multiply(hold, spots_of(0, False), (2,))
+    for copy in w_copies[:18]:
+        copy.wait()
+    sums = [acc_a, acc_b]
+    done = []
+
+    def block(pair, outer, taps=(0, 1, 2), plus=None):
+        spots = spots_of(pair, outer)
+        into = sums[len(done) % 2]
+        multiply(into, spots, taps, plus)
+        if done:
+            activate(*done[-1])
+        done.append((into, spots))
+
+    for pair in range(1, pairs):
+        block(pair, False)
+    for k in (3, 4):
+        @pl.when(halos[k][4])
+        def _(k=k):
+            halo_copy(k).start()
+    for k in (0, 1):
+        await_halo(k)
+    for pair in range(1, pairs):
+        block(pair, True)
+    await_halo(2)
+    block(0, False, (0, 1), hold)
+    for k in (3, 4):
+        await_halo(k)
 
     lane = lax.broadcasted_iota(jnp.int32, (cols // 4, 128), 1)
 
@@ -196,12 +225,14 @@
         )
 
     tx[lat] = project([(frames - 1, 0)])
+    block(0, True)
 
     @pl.when(next_ok)
     def _():
         tail_copy().start()
 
-    for f in range(lat):
+    activate(*done[-1])
+    for f in reversed(range(lat)):
         if f == 0:
             tokens = project([(0, 1), (1, 2)])
         else:
@@ -270,6 +301,8 @@
         scratch_shapes=[
             pltpu.VMEM((frames + 2, rows + 2, cols, chans), BF16),
             pltpu.VMEM((9 * chans, 3 * chans), BF16),
+            pltpu.VMEM((4 * cols, 3 * chans), F32),
+            pltpu.VMEM((4 * cols, 3 * chans), F32),
             pltpu.VMEM((4 * cols, 3 * chans), F32),
             pltpu.VMEM((frames, rows, cols, chans), BF16),
             pltpu.VMEM((3 * chans, 256), BF16),
@@ -289,7 +322,7 @@
             collective_id=0, has_side_effects=True, vmem_limit_bytes=56 * 1024 * 1024
         ),
         cost_estimate=pl.CostEstimate(flops=flops, bytes_accessed=12 << 20, transcendentals=0),
-    )(feature, conv_weight, conv_bias.reshape(1, -1), down_weight.swapaxes(3, 4), down_bias.reshape(1, -1))
+    )(feature, conv_weight, conv_bias, down_weight.swapaxes(3, 4), down_bias.reshape(1, -1))
 
 
 def solution(mesh):

time: 38.5 us -> 39.2 us (1.018)
  Pallas kernels: 35.7 us -> 37.6 us
  local copies, waits for them, and re-layouts: 2.62 us -> 1.38 us
    pallas_call x1, Pallas kernels: 35.7 us -> 37.6 us  [on_device(): pl.pallas_call(functools.partial(kernel, n_tm, n_row), out_shape=jax.Shap...]
    reshape x1 -> x0, local copies, waits for them, and re-layouts: 1.24 us -> none  [on_device(): conv_bias.reshape(1, -1)]
where the time goes in v2:
time: 39.2 us; the launch traced here: 39 us
  Pallas kernels  37.6 us (96%)
  local copies, waits for them, and re-layouts  1.38 us (4%)
    pallas_call x1, Pallas kernels, on_device(): pl.pallas_call(functools.partial(kernel, n_tm, n_row), out_shape=jax.Shap...  37.6 us
    unnamed x1, local copies, waits for them, and re-layouts  1.38 us

profile of v2, /device:TPU:0, one launch (start us, length us, event | category | flops | bytes accessed | tf_op | source)
XLA Modules:
  0.0 39.0 jit_solution(14008358125175191395)
XLA Ops:
  0.0 37.6 %shard_map.55 = f32[64,64]{1,0:T(8,128)} custom-call(bf16[4,4,128,384]{3,2,1,0:T(8,128)(2,1)} %x_ref.1, bf16[3,3,3,384,384]{4,3,2,1,0:T(8,128)(2,1)} %cw_ref.1, f32[384]{0:T(512)} %cb_ref.1, bf16[3,2,2,16,384]{4,3,2,1,0:T(8,128)(2,1)} %bitcast.2, f32[1,16]{1,0:T(1,128)} %bitcast.3), custom_call_target="tpu_custom_call" | custom-call | flops 16307453952 | bytes 12582912 | tf_op jit(solution)/shard_map/pallas_call | solution.py:296
  37.6 1.4 %copy.7 = f32[64,64]{1,0:T(8,128)} copy(f32[64,64]{1,0:T(8,128)} %shard_map.55) | data formatting | bytes 32768

commit v3 on v1

--- a/solution.py
+++ b/solution.py
@@ -72,17 +72,25 @@
                 w_copies.append(
                     pltpu.make_async_copy(
                         cw_ref.at[a, b, c],
-                        w.at[pl.ds((3 * a + b) * chans, chans), pl.ds(c * chans, chans)],
+                        w.at[a, pl.ds(b * chans, chans), pl.ds(c * chans, chans)],
                         w_sem.at[9 * a + 3 * b + c],
                     )
                 )
-                w_copies[-1].start()
+
+    for copy in w_copies[18:] + w_copies[:18]:
+        copy.start()
+
+    bias_row = jnp.broadcast_to(cb_ref[...].reshape(1, chans), (4 * cols, chans))
+    for n in range(frames):
+        acc[n, :, :chans] = jnp.zeros((4 * cols, chans), F32)
+        acc[n, :, chans : 2 * chans] = bias_row
+        acc[n, :, 2 * chans :] = jnp.zeros((4 * cols, chans), F32)
 
     targets = [goes for _, _, _, _, goes, _ in halos] + [next_ok]
     targets += [owner_of(f)[0] != row for f in range(lat)]
     pl.semaphore_wait(barrier, sum(jnp.where(goes, 1, 0) for goes in targets))
 
-    for k in range(5):
+    for k in range(3):
         @pl.when(halos[k][4])
         def _(k=k):
             halo_copy(k).start()
@@ -114,48 +122,20 @@
             wd[a * chans : (a + 1) * chans, dy * 128 : (dy + 1) * 128] = part.astype(BF16)
 
     x_copy.wait()
-    for copy in w_copies:
-        copy.wait()
 
     pairs = frames // 2
-    early = pairs - 1
     row_id = lax.broadcasted_iota(jnp.int32, (cols, chans), 0)
 
-    def await_halo(k, when):
-        @pl.when(when & halos[k][5])
-        def _():
-            halo_copy(k).wait_recv()
-
-    def conv_step(step, _):
-        await_halo(0, step == early)
-        await_halo(1, step == early)
-        await_halo(2, step == 2 * early)
-        await_halo(3, step == 2 * early + 1)
-        await_halo(4, step == 2 * early + 1)
-        is_late = step >= 2 * early
-        outer = jnp.where(is_late, step - 2 * early, (step >= early).astype(jnp.int32))
-        pair = jnp.where(is_late, 0, step - outer * early + 1)
-        first = 2 * pair
-        places = [(df, i) for df in range(2) for i in range(2)]
-        spots = [(first + df, 1 - outer if i == 0 else 2 + outer) for df, i in places]
-        pieces = []
-        for a in range(3):
-            for b in range(3):
-                pieces.append(jnp.concatenate([xs[f + a, i + b] for f, i in spots], axis=0))
-        lhs = jnp.concatenate(pieces, axis=1)
-        acc[:, : 2 * chans] = jnp.dot(lhs, w[:, : 2 * chans], preferred_element_type=F32)
-        acc[:, 2 * chans :] = jnp.dot(lhs, w[:, 2 * chans :], preferred_element_type=F32)
+    def activate(source, spots):
         for n, (f, i) in enumerate(spots):
             span = slice(n * cols, (n + 1) * cols)
-            left = pltpu.roll(acc[span, :chans], 1, 0)
-            right = pltpu.roll(acc[span, 2 * chans :], cols - 1, 0)
-            pre = acc[span, chans : 2 * chans] + cb_ref[...]
+            left = pltpu.roll(source[span, :chans], 1, 0)
+            right = pltpu.roll(source[span, 2 * chans :], cols - 1, 0)
+            pre = source[span, chans : 2 * chans]
             pre += jnp.where(row_id == 0, 0.0, left)
             pre += jnp.where(row_id == cols - 1, 0.0, right)
-            act[f, i] = (pre / (1.0 + jnp.exp(-pre))).astype(BF16)
-        return 0
-
-    lax.fori_loop(0, 2 * pairs, conv_step, 0)
+            half = 0.5 * pre
+            act[f, i] = (half + half * jnp.tanh(half)).astype(BF16)
 
     lane = lax.broadcasted_iota(jnp.int32, (cols // 4, 128), 1)
 
@@ -195,13 +175,76 @@
             device_id={"tm": tm + 1, "row": owner}, device_id_type=MESH,
         )
 
-    tx[lat] = project([(frames - 1, 0)])
-
-    @pl.when(next_ok)
-    def _():
-        tail_copy().start()
-
-    for f in range(lat):
+    early = 3 * (pairs - 1)
+    begin_late = 1 + 2 * early
+
+    def conv_step(step, _):
+        @pl.when(step == 0)
+        def _():
+            for copy in w_copies[18:]:
+                copy.wait()
+
+        @pl.when(step == 2)
+        def _():
+            for copy in w_copies[:9]:
+                copy.wait()
+
+        @pl.when(step == 3)
+        def _():
+            for copy in w_copies[9:18]:
+                copy.wait()
+
+        @pl.when(step == 1 + early)
+        def _():
+            for k in (3, 4):
+                @pl.when(halos[k][4])
+                def _(k=k):
+                    halo_copy(k).start()
+
+        for k, at in enumerate((1 + early, 1 + early, begin_late + 1, begin_late + 3, begin_late + 3)):
+            @pl.when((step == at) & halos[k][5])
+            def _(k=k):
+                halo_copy(k).wait_recv()
+
+        late = step - begin_late
+        is_late = late >= 0
+        is_first = step == 0
+        outer = jnp.where(
+            is_late, jnp.where((late == 0) | (late > 2), 1, 0), jnp.where(step > early, 1, 0)
+        )
+        turn = jnp.maximum(step - 1 - jnp.where(step > early, early, 0), 0)
+        pair = jnp.where(is_late | is_first, 0, 1 + turn // 3)
+        tap = jnp.where(
+            is_late,
+            jnp.where(late == 0, 2, jnp.where(late > 2, late - 3, late - 1)),
+            jnp.where(is_first, 2, (turn + 2) % 3),
+        )
+        spots = [(2 * pair + df, i) for df in range(2) for i in (1 - outer, rows - 2 + outer)]
+        lhs = jnp.concatenate(
+            [jnp.concatenate([xs[f + tap, i + b] for f, i in spots], axis=0) for b in range(3)],
+            axis=1,
+        )
+        into = acc.at[2 * pair + outer]
+        for lanes in (slice(0, 2 * chans), slice(2 * chans, 3 * chans)):
+            into[:, lanes] += jnp.dot(lhs, w[tap, :, lanes], preferred_element_type=F32)
+
+        @pl.when(tap == 1)
+        def _():
+            activate(into, spots)
+
+        @pl.when(step == begin_late)
+        def _():
+            tx[lat] = project([(frames - 1, 0)])
+
+            @pl.when(next_ok)
+            def _():
+                tail_copy().start()
+
+        return 0
+
+    lax.fori_loop(0, 6 * pairs, conv_step, 0)
+
+    for f in reversed(range(lat)):
         if f == 0:
             tokens = project([(0, 1), (1, 2)])
         else:
@@ -269,8 +312,8 @@
         out_specs=vmem,
         scratch_shapes=[
             pltpu.VMEM((frames + 2, rows + 2, cols, chans), BF16),
-            pltpu.VMEM((9 * chans, 3 * chans), BF16),
-            pltpu.VMEM((4 * cols, 3 * chans), F32),
+            pltpu.VMEM((3, 3 * chans, 3 * chans), BF16),
+            pltpu.VMEM((frames, 4 * cols, 3 * chans), F32),
             pltpu.VMEM((frames, rows, cols, chans), BF16),
             pltpu.VMEM((3 * chans, 256), BF16),
             pltpu.VMEM((2, rows * cols, 128), F32),
@@ -289,7 +332,7 @@
             collective_id=0, has_side_effects=True, vmem_limit_bytes=56 * 1024 * 1024
         ),
         cost_estimate=pl.CostEstimate(flops=flops, bytes_accessed=12 << 20, transcendentals=0),
-    )(feature, conv_weight, conv_bias.reshape(1, -1), down_weight.swapaxes(3, 4), down_bias.reshape(1, -1))
+    )(feature, conv_weight, conv_bias, down_weight.swapaxes(3, 4), down_bias.reshape(1, -1))
 
 
 def solution(mesh):

time: 38.5 us -> 39.2 us (1.018)
  Pallas kernels: 35.7 us -> 37.6 us
  local copies, waits for them, and re-layouts: 2.62 us -> 1.38 us
    pallas_call x1, Pallas kernels: 35.7 us -> 37.6 us  [on_device(): pl.pallas_call(functools.partial(kernel, n_tm, n_row), out_shape=jax.Shap...]
    reshape x1 -> x0, local copies, waits for them, and re-layouts: 1.24 us -> none  [on_device(): conv_bias.reshape(1, -1)]
where the time goes in v3:
time: 39.2 us; the launch traced here: 39 us
  Pallas kernels  37.6 us (96%)
  local copies, waits for them, and re-layouts  1.38 us (4%)
    pallas_call x1, Pallas kernels, on_device(): pl.pallas_call(functools.partial(kernel, n_tm, n_row), out_shape=jax.Shap...  37.6 us
    unnamed x1, local copies, waits for them, and re-layouts  1.38 us

profile of v3, /device:TPU:0, one launch (start us, length us, event | category | flops | bytes accessed | tf_op | source)
XLA Modules:
  0.0 39.0 jit_solution(12102544751431274211)
XLA Ops:
  0.0 37.6 %shard_map.55 = f32[64,64]{1,0:T(8,128)} custom-call(bf16[4,4,128,384]{3,2,1,0:T(8,128)(2,1)} %x_ref.1, bf16[3,3,3,384,384]{4,3,2,1,0:T(8,128)(2,1)} %cw_ref.1, f32[384]{0:T(512)} %cb_ref.1, bf16[3,2,2,16,384]{4,3,2,1,0:T(8,128)(2,1)} %bitcast.2, f32[1,16]{1,0:T(1,128)} %bitcast.3), custom_call_target="tpu_custom_call" | custom-call | flops 16307453952 | bytes 12582912 | tf_op jit(solution)/shard_map/pallas_call | solution.py:308
  37.6 1.4 %copy.7 = f32[64,64]{1,0:T(8,128)} copy(f32[64,64]{1,0:T(8,128)} %shard_map.55) | data formatting | bytes 32768
